TPU v7x, 32 devices: a whole 2x2x4 slice. The times are simulated.
32 devices in a mesh: frame: 8 (over z, y), chan: 4 (over x, core).
Axes of the slice: x: 2, y: 2, z: 4, core: 2. Of those that a mesh axis runs over, the one named last changes fastest.
Arguments:
- inputs: bfloat16 [1536, 3072], P('chan', 'frame'), may hold values from -6 to 6
- norm_gain: float32 [1536], replicated, may hold values from 0.5 to 2
- norm_bias: float32 [1536], replicated, may hold values from -3 to 3
- value_weight: bfloat16 [1536, 1536], P('chan'), may hold values from -0.15625 to 0.15625
- gate_weight: bfloat16 [1536, 1536], P('chan'), may hold values from -0.15625 to 0.15625
- conv_kernel: float32 [31, 1536], P(None, 'chan'), may hold values from -1 to 1
- project_weight: bfloat16 [1536, 1536], P('chan'), may hold values from -0.15625 to 0.15625
- frame_mask: int32 [3072], P('frame'), may hold values 0 or 1
- upstream: bfloat16 [1536, 3072], P('chan', 'frame'), may hold values from -6 to 6
Outputs:
- inputs_grad: bfloat16 [1536, 3072], P('chan', 'frame')
- value_grad: float32 [1536, 1536], P('chan', 'frame')
- gate_grad: float32 [1536, 1536], P('chan', 'frame')
- project_grad: float32 [1536, 1536], P('chan', 'frame')
- kernel_grad: float32 [31, 1536], P(None, 'chan')
- gain_grad: float32 [1536], P('chan')
- bias_grad: float32 [1536], P('chan')
All inputs are finite; a program needn't handle non-finite values. No bound on the sum of `frame_mask` on one device may be relied on, other than what follows from the above.
Results may differ from a plain program's by a relative error of at most 0.025.
Values may be sent and summed in bfloat16 or wider, within the bound.
A program may use at most 64 MiB of HBM per device.

v0:
```python
import jax
import jax.numpy as jnp
from jax import lax
from jax.sharding import PartitionSpec as P

eps = 1e-05


def padded_2(cells, sides, width):
    for axis, dim in sides:
        count = lax.axis_size(axis)
        ends = count - 1
        head = lax.slice_in_dim(cells, 0, width, axis=dim)
        tail = lax.slice_in_dim(cells, cells.shape[dim] - width, cells.shape[dim], axis=dim)
        cells = jnp.concatenate(
            [
                lax.ppermute(tail, axis, [(i, (i + 1) % count) for i in range(ends)]),
                cells,
                lax.ppermute(head, axis, [((i + 1) % count, i) for i in range(ends)]),
            ],
            axis=dim,
        )
    return cells


def on_device(
    inputs,
    norm_gain,
    norm_bias,
    value_weight,
    gate_weight,
    conv_kernel,
    project_weight,
    frame_mask,
    upstream,
):
    chan_width = inputs.shape[0]
    frame_rows = inputs.shape[1]
    model_width = value_weight.shape[1]
    taps = conv_kernel.shape[0]
    reach = taps // 2
    chan_index = lax.axis_index("chan")
    offset = chan_index * chan_width
    full_inputs = lax.all_gather(inputs, "chan", axis=0, tiled=True)
    x_float = full_inputs.astype(jnp.float32)
    row_mean = jnp.mean(x_float, axis=0, keepdims=True)
    row_var = jnp.mean(x_float * x_float, axis=0, keepdims=True) - row_mean * row_mean
    inv_std = lax.rsqrt(row_var + eps)
    centred = (x_float - row_mean) * inv_std
    normed = (centred * norm_gain[:, None] + norm_bias[:, None]).astype(jnp.bfloat16)
    centred_local = lax.dynamic_slice_in_dim(centred, offset, chan_width, 0)
    gain_local = lax.dynamic_slice_in_dim(norm_gain, offset, chan_width, 0)[:, None]
    value_proj = jnp.dot(value_weight, normed, preferred_element_type=jnp.float32)
    gate_proj = jnp.dot(gate_weight, normed, preferred_element_type=jnp.float32)
    gate_sig = jax.nn.sigmoid(gate_proj)
    keep = frame_mask.astype(jnp.float32)[None, :]
    glu_out = (value_proj * gate_sig * keep).astype(jnp.bfloat16)
    padded = padded_2(glu_out, (("frame", 1),), reach)
    conv_out = jnp.zeros((chan_width, frame_rows), jnp.float32)
    for k in range(taps):
        conv_out = conv_out + conv_kernel[k][:, None] * padded[:, k : k + frame_rows].astype(
            jnp.float32
        )
    conv_sig = jax.nn.sigmoid(conv_out)
    activated = (conv_out * conv_sig).astype(jnp.bfloat16)
    full_grads = lax.all_gather(upstream, "chan", axis=0, tiled=True)
    act_grad = jnp.dot(project_weight, full_grads, preferred_element_type=jnp.float32).astype(
        jnp.bfloat16
    )
    project_part = lax.dot_general(
        activated, full_grads, (((1,), (1,)), ((), ())), preferred_element_type=jnp.float32
    )
    conv_grad = (
        act_grad.astype(jnp.float32) * (conv_sig + conv_out * conv_sig * (1.0 - conv_sig))
    ).astype(jnp.bfloat16)
    back_pad = padded_2(conv_grad, (("frame", 1),), reach)
    grad_float = conv_grad.astype(jnp.float32)
    glu_grad = jnp.zeros((chan_width, frame_rows), jnp.float32)
    kernel_rows = []
    for k in range(taps):
        glu_grad = glu_grad + conv_kernel[k][:, None] * back_pad[
            :, 2 * reach - k : 2 * reach - k + frame_rows
        ].astype(jnp.float32)
        kernel_rows.append(
            jnp.sum(grad_float * padded[:, k : k + frame_rows].astype(jnp.float32), axis=1)
        )
    kernel_part = jnp.stack(kernel_rows)
    glu_grad = glu_grad * keep
    value_back = (glu_grad * gate_sig).astype(jnp.bfloat16)
    gate_back = (glu_grad * value_proj * gate_sig * (1.0 - gate_sig)).astype(jnp.bfloat16)
    value_part = lax.dot_general(
        value_back, normed, (((1,), (1,)), ((), ())), preferred_element_type=jnp.float32
    )
    gate_part = lax.dot_general(
        gate_back, normed, (((1,), (1,)), ((), ())), preferred_element_type=jnp.float32
    )
    result = lax.dot_general(
        value_weight, value_back, (((0,), (0,)), ((), ())), preferred_element_type=jnp.float32
    )
    normed_grad = lax.psum_scatter(
        (
            result
            + lax.dot_general(
                gate_weight, gate_back, (((0,), (0,)), ((), ())), preferred_element_type=jnp.float32
            )
        ).astype(jnp.bfloat16),
        "chan",
        scatter_dimension=0,
        tiled=True,
    ).astype(jnp.float32)
    scaled_here = normed_grad * gain_local
    first_sum, second_sum = lax.psum(
        (
            jnp.sum(scaled_here, axis=0, keepdims=True),
            jnp.sum(scaled_here * centred_local, axis=0, keepdims=True),
        ),
        "chan",
    )
    first_sum = first_sum / model_width
    second_sum = second_sum / model_width
    scaled = normed_grad * gain_local
    inputs_grad = (
        upstream.astype(jnp.float32) + inv_std * (scaled - first_sum - centred_local * second_sum)
    ).astype(jnp.bfloat16)
    gain_part = jnp.sum(normed_grad * centred_local, axis=1)
    bias_part = jnp.sum(normed_grad, axis=1)
    value_grad, gate_grad, project_grad = (
        lax.psum_scatter(
            value_part.astype(jnp.bfloat16), "frame", scatter_dimension=1, tiled=True
        ).astype(jnp.float32),
        lax.psum_scatter(
            gate_part.astype(jnp.bfloat16), "frame", scatter_dimension=1, tiled=True
        ).astype(jnp.float32),
        lax.psum_scatter(
            project_part.astype(jnp.bfloat16), "frame", scatter_dimension=1, tiled=True
        ).astype(jnp.float32),
    )
    kernel_grad, gain_grad, bias_grad = lax.psum((kernel_part, gain_part, bias_part), "frame")
    return (inputs_grad, value_grad, gate_grad, project_grad, kernel_grad, gain_grad, bias_grad)


def solution(mesh):
    return jax.shard_map(
        on_device,
        mesh=mesh,
        in_specs=(
            P("chan", "frame"),
            P(),
            P(),
            P("chan", None),
            P("chan", None),
            P(None, "chan"),
            P("chan", None),
            P("frame"),
            P("chan", "frame"),
        ),
        out_specs=(
            P("chan", "frame"),
            P("chan", "frame"),
            P("chan", "frame"),
            P("chan", "frame"),
            P(None, "chan"),
            P("chan"),
            P("chan"),
        ),
        check_vma=False,
    )
```

profile of v0, /device:TPU:9, one launch (start us, length us, event | category | flops | bytes accessed | tf_op | source)
XLA Modules:
  0.0 286.3 jit_solution(720755201113593243)
XLA Ops:
  7.2 2.0 copy.22
  9.3 0.7 all-gather.5.cloned.1.call-update
  10.1 0.7 convert_element_type.286
  10.8 1.9 slice_reduce_fusion.30
  12.7 16.5 %all-gather.3.cloned.1.call-done = bf16[1536,384]{0,1:T(8,128)(2,1)} async-done(((bf16[384,384]{0,1:T(8,128)(2,1)}), bf16[1536,384]{0,1:T(8,128)(2,1)}) %all-gather.3.cloned.1.call-update) | async-done | bytes 1179664 | tf_op jit(solution)/shard_map/all_gather | solution.py:44
  29.2 1.7 convert_reduce_fusion
  31.0 3.2 %fusion.6 = f32[384,384]{0,1:T(8,128)} fusion(bf16[384,1536]{1,0:T(8,128)(2,1)S(1)} %copy-done.8, f32[1536]{0:T(1024)} %param.11, f32[1536]{0:T(1024)} %param.10, f32[384]{0:T(512)S(1)} %get-tuple-element.101, f32[384]{0:T(512)S(1)} %get-tuple-element.100, bf16[1536,384]{0,1:T(8,128)(2,1)} %all-gather.3.cloned.1.call-done), kind=kOutput, calls=%fused_computation.103 | convolution fusion | flops 456966144 | bytes 2964480 | tf_op jit(solution)/shard_map/dot_general | solution.py:54
  34.2 1.3 copy.24
  35.7 2.4 fusion.97
  38.1 3.1 %collective-permute-start = (bf16[384,15]{0,1:T(8,128)(2,1)S(1)}, bf16[384,15]{0,1:T(8,128)(2,1)S(1)}, u32[]{:S(2)}, u32[]{:S(2)}) collective-permute-start(bf16[384,15]{0,1:T(8,128)(2,1)S(1)} %get-tuple-element.98), channel_id=1, source_target_pairs={{0,4},{4,8},{8,12},{12,16},{16,20},{20,24},{24,28},{1,5},{5,9},{9,... | collective-permute-start | bytes 34568 | tf_op jit(solution)/shard_map/ppermute | solution.py:17
  41.2 3.1 %collective-permute-start.1 = (bf16[384,15]{0,1:T(8,128)(2,1)S(1)}, bf16[384,15]{0,1:T(8,128)(2,1)S(1)}, u32[]{:S(2)}, u32[]{:S(2)}) collective-permute-start(bf16[384,15]{0,1:T(8,128)(2,1)S(1)} %get-tuple-element.99), channel_id=1, source_target_pairs={{4,0},{8,4},{12,8},{16,12},{20,16},{24,20},{28,24},{5,1},{9,5},{13... | collective-permute-start | bytes 34568 | tf_op jit(solution)/shard_map/ppermute | solution.py:19
  44.3 1.0 slice_reduce_fusion.29
  45.4 0.7 collective-permute-done.1
  46.2 3.4 %fusion.42 = f32[384,384]{0,1:T(8,128)} fusion(bf16[384,384]{0,1:T(8,128)(2,1)S(1)} %get-tuple-element.102, bf16[384,15]{0,1:T(8,128)(2,1)S(1)} %collective-permute-done.1, bf16[384,15]{0,1:T(8,128)(2,1)S(1)} %collective-permute-done, f32[384]{0:T(512)S(1)} %get-tuple-element.87, f32[384]{0:T(512)S(1)} %get-tuple-element.88, f32[384]{0:T(512)S(1)} %copy-done.14, ...), kind=kLoop, calls=%fused_computation.175 | loop fusion | flops 26836992 | bytes 955392 | tf_op jit(solution)/shard_map/add | solution.py:61
  49.6 3.4 %convolution_convert_fusion = bf16[384,1536]{0,1:T(8,128)(2,1)} fusion(bf16[1536,384]{1,0:T(8,128)(2,1)} %all-gather.5.cloned.1.call-done, f32[384,384]{0,1:T(8,128)} %fusion.42), kind=kOutput, calls=%fused_computation.37 | convolution fusion | flops 454311936 | bytes 2949120 | tf_op jit(solution)/shard_map/dot_general | solution.py:70
  53.1 3.8 %fusion.78 = (f32[384]{0:T(512)}, f32[384]{0:T(512)}, f32[384]{0:T(512)}, f32[384]{0:T(512)}, f32[384]{0:T(512)}, /*index=5*/f32[384]{0:T(512)}, bf16[384,384]{0,1:T(8,128)(2,1)S(1)}) fusion(bf16[384,384]{0,1:T(8,128)(2,1)S(1)} %get-tuple-element.102, bf16[384,15]{0,1:T(8,128)(2,1)S(1)} %collective-permute-done, f32[384,384]{0,1:T(8,128)} %fusion.42, ...), kind=kOutput, calls=%fused_computation.211 | convolution fusion | flops 460060416 | bytes 3559680 | tf_op jit(solution)/shard_map/dot_general | solution.py:67
  57.0 3.6 %collective-permute-start.2 = (bf16[384,15]{0,1:T(8,128)(2,1)S(1)}, bf16[384,15]{0,1:T(8,128)(2,1)S(1)}, u32[]{:S(2)}, u32[]{:S(2)}) collective-permute-start(bf16[384,15]{0,1:T(8,128)(2,1)S(1)} %get-tuple-element.96), channel_id=1, source_target_pairs={{4,0},{8,4},{12,8},{16,12},{20,16},{24,20},{28,24},{5,1},{9,5},{13... | collective-permute-start | bytes 34568 | tf_op jit(solution)/shard_map/ppermute | solution.py:19
  60.6 1.9 collective-permute-start.3
  62.5 3.4 %collective-permute-done.3 = bf16[384,15]{0,1:T(8,128)(2,1)S(1)} collective-permute-done((bf16[384,15]{0,1:T(8,128)(2,1)S(1)}, bf16[384,15]{0,1:T(8,128)(2,1)S(1)}, u32[]{:S(2)}, u32[]{:S(2)}) %collective-permute-start.3) | collective-permute-done | bytes 11552 | tf_op jit(solution)/shard_map/ppermute | solution.py:17
  65.9 4.8 %fusion.100 = (bf16[384,384]{0,1:T(8,128)(2,1)S(1)}, f32[384,384]{0,1:T(8,128)S(1)}) fusion(f32[384,384]{1,0:T(8,128)S(1)} %copy.24, f32[384,384]{0,1:T(8,128)S(1)} %copy-done.12, f32[384]{0:T(512)S(1)} %copy-done.35, bf16[384,384]{0,1:T(8,128)(2,1)S(1)} %get-tuple-element.104, bf16[384,15]{0,1:T(8,128)(2,1)S(1)} %collective-permute-done.3, ...), kind=kLoop, calls=%fused_computation.237 | loop fusion | flops 27721728 | bytes 2431488 | tf_op jit(solution)/shard_map/convert_element_type | solution.py:90
  70.8 0.8 fusion.166
  71.6 0.6 copy-done.9
  72.2 0.8 fusion.1
  73.1 1.4 copy.27
  74.6 3.2 %convolution_convert_fusion.2 = bf16[384,1536]{0,1:T(8,128)(2,1)} fusion(bf16[384,384]{0,1:T(8,128)(2,1)} %copy-done.11, f32[1536]{0:T(1024)} %param.11, f32[1536]{0:T(1024)} %param.10, f32[384]{0:T(512)S(1)} %copy-done.33, f32[384]{0:T(512)} %copy-done.36, bf16[1536,384]{0,1:T(8,128)(2,1)S(1)} %copy-done.5), kind=kOutput, calls=%fused_computation.39 | convolution fusion | flops 457113600 | bytes 2669568 | tf_op jit(solution)/shard_map/dot_general | solution.py:91
  78.1 2.1 convolution_convert_fusion.1
  80.2 0.9 copy.21
  81.2 1.7 fusion.3
  82.9 3.5 %fusion.79 = (f32[384]{0:T(512)S(1)}, f32[384]{0:T(512)S(1)}, f32[384]{0:T(512)S(1)}, f32[384]{0:T(512)S(1)}, f32[384]{0:T(512)S(1)}, /*index=5*/f32[384]{0:T(51...) fusion(bf16[384,384]{0,1:T(8,128)(2,1)} %copy-done.1, bf16[384,384]{0,1:T(8,128)(2,1)} %copy-done.3, ...), kind=kLoop, calls=%fused_computation.212 | loop fusion | flops 8106624 | bytes 615168 | tf_op jit(solution)/shard_map/reduce_sum | solution.py:85
  91.6 3.5 %fusion.95 = (f32[384]{0:T(512)S(1)}, f32[384]{0:T(512)S(1)}, f32[384]{0:T(512)S(1)}, f32[384]{0:T(512)S(1)}, f32[384]{0:T(512)S(1)}, /*index=5*/f32[384]{0:T(51...) fusion(bf16[384,384]{0,1:T(8,128)(2,1)} %copy-done.1, bf16[384,15]{0,1:T(8,128)(2,1)S(1)} %collective-permute-done.1, ...), kind=kLoop, calls=%fused_computation.228 | loop fusion | flops 8106624 | bytes 615168 | tf_op jit(solution)/shard_map/reduce_sum | solution.py:85
  97.5 0.6 stack.116
  101.0 0.6 stack.122
  103.8 0.6 stack.109
  106.7 5.3 %stack.127 = f32[31,384]{1,0:T(8,128)} concatenate(f32[1,384]{1,0:T(1,128)} %stack.96, f32[1,384]{1,0:T(1,128)} %stack.97, f32[1,384]{1,0:T(1,128)} %stack.98, f32[1,384]{1,0:T(1,128)} %stack.99, f32[1,384]{1,0:T(1,128)} %stack.100, f32[1,384]{1,0:T(1,128)} %stack.101, f32[1,384]{1,0:T(1,128)} %stack.102, f32[1,384]{1,0:T(1,128)} %stack.103, f32[1,384]{1,0:T(1,128)} %stack.104, ...), dimensions={0} | concatenate | bytes 95232 | tf_op jit(solution)/shard_map/stack | solution.py:87
  112.1 4.2 %reduce-scatter.11.cloned.1.call-done = bf16[384,192]{0,1:T(8,128)(2,1)} async-done(((bf16[384,1536]{0,1:T(8,128)(2,1)}), bf16[384,192]{0,1:T(8,128)(2,1)}) %reduce-scatter.11.cloned.1.call-update) | async-done | bytes 147472 | tf_op jit(solution)/shard_map/reduce_scatter | solution.py:134
  116.3 1.6 convert_element_type.363
  117.9 27.6 %reduce-scatter.13.cloned.1.call-done = bf16[384,384]{1,0:T(8,128)(2,1)} async-done(((bf16[1536,384]{1,0:T(8,128)(2,1)}), bf16[384,384]{1,0:T(8,128)(2,1)}) %reduce-scatter.13.cloned.1.call-update) | async-done | bytes 294928
  145.5 1.8 copy.28
  147.4 1.8 fusion.48
  149.8 6.3 %all-reduce.1 = (f32[1,384]{1,0:T(1,128)}, f32[1,384]{1,0:T(1,128)}) all-reduce(f32[1,384]{1,0:T(1,128)S(1)} %broadcast_in_dim.5, f32[1,384]{1,0:T(1,128)} %broadcast_in_dim.4), channel_id=1, replica_groups=mesh['frame'=8,'chan'=4] {'chan'}, use_global_device_ids=true, to_apply=%region_6.0 | all-reduce | flops 768 | bytes 6144 | tf_op jit(solution)/shard_map/psum | solution.py:112
  156.1 0.7 multiply_reduce_fusion
  156.8 2.0 fusion.46
  158.8 1.8 copy.25
  160.7 50.4 %reduce-scatter.7.cloned.1.call-done = bf16[384,192]{0,1:T(8,128)(2,1)} async-done(((bf16[384,1536]{0,1:T(8,128)(2,1)}), bf16[384,192]{0,1:T(8,128)(2,1)}) %reduce-scatter.7.cloned.1.call-update) | async-done | bytes 147472 | tf_op jit(solution)/shard_map/reduce_scatter | solution.py:128
  211.1 1.6 convert_element_type.358
  212.7 27.9 %all-reduce = (f32[31,384]{1,0:T(8,128)}, f32[384]{0:T(512)}, f32[384]{0:T(512)}) all-reduce(f32[31,384]{1,0:T(8,128)} %stack.127, f32[384]{0:T(512)S(1)} %get-tuple-element.21, f32[384]{0:T(512)} %get-tuple-element.57), channel_id=1, replica_groups=mesh['frame'=8,'chan'=4] {'frame'}, use_global_device_ids=true, to_apply=%region_41.0 | all-reduce | flops 12672 | bytes 101376 | tf_op jit(solution)/shard_map/psum | solution.py:138
  240.6 37.2 %reduce-scatter.9.cloned.1.call-done = bf16[384,192]{0,1:T(8,128)(2,1)} async-done(((bf16[384,1536]{0,1:T(8,128)(2,1)}), bf16[384,192]{0,1:T(8,128)(2,1)}) %reduce-scatter.9.cloned.1.call-update) | async-done | bytes 147472 | tf_op jit(solution)/shard_map/reduce_scatter | solution.py:131
  277.8 1.6 convert_element_type.360
  (141 shorter events, 16.4 us)
Async XLA Ops:
  7.2 28.3 %copy-start = (bf16[384,1536]{1,0:T(8,128)(2,1)S(1)}, bf16[384,1536]{1,0:T(8,128)(2,1)}, u32[]{:S(2)}) copy-start(bf16[384,1536]{1,0:T(8,128)(2,1)} %param.12) | copy-start | bytes 3538948
  7.2 23.8 %copy-start.8 = (bf16[384,1536]{1,0:T(8,128)(2,1)S(1)}, bf16[384,1536]{1,0:T(8,128)(2,1)}, u32[]{:S(2)}) copy-start(bf16[384,1536]{1,0:T(8,128)(2,1)} %param.13) | copy-start | bytes 3538948
  7.2 22.0 %all-gather.3.cloned.1.call-start = ((), (), s32[]{:S(2)}) async-start(), calls=%async_computation.4 | async-start | bytes 1474560 | tf_op jit(solution)/shard_map/all_gather | solution.py:44
  9.3 40.4 %all-gather.5.cloned.1.call-start = ((), (), s32[]{:S(2)}) async-start(), calls=%async_computation.5 | async-start | bytes 1474560 | tf_op jit(solution)/shard_map/all_gather | solution.py:66
  10.0 106.3 %reduce-scatter.11.cloned.1.call-start = ((), (), s32[]{:S(2)}) async-start(), calls=%async_computation.8 | async-start | bytes 1327104 | tf_op jit(solution)/shard_map/reduce_scatter | solution.py:134
  10.7 24.7 %copy-start.34 = (f32[384]{0:T(512)}, f32[384]{0:T(512)S(1)}, u32[]{:S(2)}) copy-start(f32[384]{0:T(512)S(1)} %convert_element_type.286) | copy-start | bytes 4612
  30.9 4.5 %copy-start.32 = (f32[384]{0:T(512)}, f32[384]{0:T(512)S(1)}, u32[]{:S(2)}) copy-start(f32[384]{0:T(512)S(1)} %get-tuple-element.101) | copy-start | bytes 4612
  30.9 4.5 %copy-start.36 = (f32[384]{0:T(512)}, f32[384]{0:T(512)S(1)}, u32[]{:S(2)}) copy-start(f32[384]{0:T(512)S(1)} %get-tuple-element.100) | copy-start | bytes 4612
  31.0 4.5 %copy-start.5 = (bf16[1536,384]{0,1:T(8,128)(2,1)S(1)}, bf16[1536,384]{0,1:T(8,128)(2,1)}, u32[]{:S(2)}) copy-start(bf16[1536,384]{0,1:T(8,128)(2,1)} %all-gather.3.cloned.1.call-done) | copy-start | bytes 3538948
  35.5 10.5 %copy-start.14 = (f32[384]{0:T(512)S(1)}, f32[384]{0:T(512)}, u32[]{:S(2)}) copy-start(f32[384]{0:T(512)} %get-tuple-element.59) | copy-start | bytes 4612
  35.5 10.5 %copy-start.15 = (f32[384]{0:T(512)S(1)}, f32[384]{0:T(512)}, u32[]{:S(2)}) copy-start(f32[384]{0:T(512)} %get-tuple-element.60) | copy-start | bytes 4612
  35.6 10.5 %copy-start.16 = (f32[384]{0:T(512)S(1)}, f32[384]{0:T(512)}, u32[]{:S(2)}) copy-start(f32[384]{0:T(512)} %get-tuple-element.61) | copy-start | bytes 4612
  35.6 10.5 %copy-start.17 = (f32[384]{0:T(512)S(1)}, f32[384]{0:T(512)}, u32[]{:S(2)}) copy-start(f32[384]{0:T(512)} %get-tuple-element.62) | copy-start | bytes 4612
  35.6 10.5 %copy-start.18 = (f32[384]{0:T(512)S(1)}, f32[384]{0:T(512)}, u32[]{:S(2)}) copy-start(f32[384]{0:T(512)} %get-tuple-element.63) | copy-start | bytes 4612
  35.6 10.5 %copy-start.19 = (f32[384]{0:T(512)S(1)}, f32[384]{0:T(512)}, u32[]{:S(2)}) copy-start(f32[384]{0:T(512)} %get-tuple-element.64) | copy-start | bytes 4612
  35.6 10.5 %copy-start.20 = (f32[384]{0:T(512)S(1)}, f32[384]{0:T(512)}, u32[]{:S(2)}) copy-start(f32[384]{0:T(512)} %get-tuple-element.65) | copy-start | bytes 4612
  35.6 10.5 %copy-start.21 = (f32[384]{0:T(512)S(1)}, f32[384]{0:T(512)}, u32[]{:S(2)}) copy-start(f32[384]{0:T(512)} %get-tuple-element.66) | copy-start | bytes 4612
  35.6 10.5 %copy-start.22 = (f32[384]{0:T(512)S(1)}, f32[384]{0:T(512)}, u32[]{:S(2)}) copy-start(f32[384]{0:T(512)} %get-tuple-element.67) | copy-start | bytes 4612
  35.6 10.5 %copy-start.23 = (f32[384]{0:T(512)S(1)}, f32[384]{0:T(512)}, u32[]{:S(2)}) copy-start(f32[384]{0:T(512)} %get-tuple-element.68) | copy-start | bytes 4612
  35.6 10.5 %copy-start.24 = (f32[384]{0:T(512)S(1)}, f32[384]{0:T(512)}, u32[]{:S(2)}) copy-start(f32[384]{0:T(512)} %get-tuple-element.69) | copy-start | bytes 4612
  35.6 10.5 %copy-start.25 = (f32[384]{0:T(512)S(1)}, f32[384]{0:T(512)}, u32[]{:S(2)}) copy-start(f32[384]{0:T(512)} %get-tuple-element.70) | copy-start | bytes 4612
  35.7 10.5 %copy-start.26 = (f32[384]{0:T(512)S(1)}, f32[384]{0:T(512)}, u32[]{:S(2)}) copy-start(f32[384]{0:T(512)} %get-tuple-element.71) | copy-start | bytes 4612
  35.7 10.5 %copy-start.27 = (f32[384]{0:T(512)S(1)}, f32[384]{0:T(512)}, u32[]{:S(2)}) copy-start(f32[384]{0:T(512)} %get-tuple-element.72) | copy-start | bytes 4612
  35.7 10.5 %copy-start.28 = (f32[384]{0:T(512)S(1)}, f32[384]{0:T(512)}, u32[]{:S(2)}) copy-start(f32[384]{0:T(512)} %get-tuple-element.73) | copy-start | bytes 4612
  35.7 10.5 %copy-start.29 = (f32[384]{0:T(512)S(1)}, f32[384]{0:T(512)}, u32[]{:S(2)}) copy-start(f32[384]{0:T(512)} %get-tuple-element.74) | copy-start | bytes 4612
  35.7 10.5 %copy-start.30 = (f32[384]{0:T(512)S(1)}, f32[384]{0:T(512)}, u32[]{:S(2)}) copy-start(f32[384]{0:T(512)} %get-tuple-element.75) | copy-start | bytes 4612
  35.7 10.5 %copy-start.31 = (f32[384]{0:T(512)S(1)}, f32[384]{0:T(512)}, u32[]{:S(2)}) copy-start(f32[384]{0:T(512)} %get-tuple-element.76) | copy-start | bytes 4612
  38.1 15.0 %copy-start.3 = (bf16[384,384]{0,1:T(8,128)(2,1)}, bf16[384,384]{0,1:T(8,128)(2,1)S(1)}, u32[]{:S(2)}) copy-start(bf16[384,384]{0,1:T(8,128)(2,1)S(1)} %get-tuple-element.102) | copy-start | bytes 884740
  38.1 7.2 %collective-permute-start = (bf16[384,15]{0,1:T(8,128)(2,1)S(1)}, bf16[384,15]{0,1:T(8,128)(2,1)S(1)}, u32[]{:S(2)}, u32[]{:S(2)}) collective-permute-start(bf16[384,15]{0,1:T(8,128)(2,1)S(1)} %get-tuple-element.98), channel_id=1, source_target_pairs={{0,4},{4,8},{8,12},{12,16},{16,20},{20,24},{24,28},{1,5},{5,9},{9,... | collective-permute-start | bytes 34568 | tf_op jit(solution)/shard_map/ppermute | solution.py:17
  41.2 4.8 %collective-permute-start.1 = (bf16[384,15]{0,1:T(8,128)(2,1)S(1)}, bf16[384,15]{0,1:T(8,128)(2,1)S(1)}, u32[]{:S(2)}, u32[]{:S(2)}) collective-permute-start(bf16[384,15]{0,1:T(8,128)(2,1)S(1)} %get-tuple-element.99), channel_id=1, source_target_pairs={{4,0},{8,4},{12,8},{16,12},{20,16},{24,20},{28,24},{5,1},{9,5},{13... | collective-permute-start | bytes 34568 | tf_op jit(solution)/shard_map/ppermute | solution.py:19
  45.4 7.8 %copy-start.13 = (bf16[384,15]{0,1:T(8,128)(2,1)}, bf16[384,15]{0,1:T(8,128)(2,1)S(1)}, u32[]{:S(2)}) copy-start(bf16[384,15]{0,1:T(8,128)(2,1)S(1)} %collective-permute-done) | copy-start | bytes 34564
  53.0 12.9 %copy-start.35 = (f32[384]{0:T(512)S(1)}, f32[384]{0:T(512)}, u32[]{:S(2)}) copy-start(f32[384]{0:T(512)} %copy-done.34) | copy-start | bytes 4612
  53.1 92.5 %reduce-scatter.13.cloned.1.call-start = ((), (), s32[]{:S(2)}) async-start(), calls=%async_computation.9 | async-start | bytes 1474560
  53.1 12.8 %copy-start.12 = (f32[384,384]{0,1:T(8,128)S(1)}, f32[384,384]{0,1:T(8,128)}, u32[]{:S(2)}) copy-start(f32[384,384]{0,1:T(8,128)} %get-tuple-element.103) | copy-start | bytes 1769476
  57.0 14.6 %copy-start.1 = (bf16[384,384]{0,1:T(8,128)(2,1)}, bf16[384,384]{0,1:T(8,128)(2,1)S(1)}, u32[]{:S(2)}) copy-start(bf16[384,384]{0,1:T(8,128)(2,1)S(1)} %get-tuple-element.104) | copy-start | bytes 884740
  57.0 5.6 %collective-permute-start.2 = (bf16[384,15]{0,1:T(8,128)(2,1)S(1)}, bf16[384,15]{0,1:T(8,128)(2,1)S(1)}, u32[]{:S(2)}, u32[]{:S(2)}) collective-permute-start(bf16[384,15]{0,1:T(8,128)(2,1)S(1)} %get-tuple-element.96), channel_id=1, source_target_pairs={{4,0},{8,4},{12,8},{16,12},{20,16},{24,20},{28,24},{5,1},{9,5},{13... | collective-permute-start | bytes 34568 | tf_op jit(solution)/shard_map/ppermute | solution.py:19
  60.6 5.3 %collective-permute-start.3 = (bf16[384,15]{0,1:T(8,128)(2,1)S(1)}, bf16[384,15]{0,1:T(8,128)(2,1)S(1)}, u32[]{:S(2)}, u32[]{:S(2)}) collective-permute-start(bf16[384,15]{0,1:T(8,128)(2,1)S(1)} %get-tuple-element.97), channel_id=1, source_target_pairs={{0,4},{4,8},{8,12},{12,16},{16,20},{20,24},{24,28},{1,5},{5,9},{9,... | collective-permute-start | bytes 34568 | tf_op jit(solution)/shard_map/ppermute | solution.py:17
  74.5 3.5 %copy-start.7 = (bf16[384,384]{0,1:T(8,128)(2,1)S(1)}, bf16[384,384]{0,1:T(8,128)(2,1)}, u32[]{:S(2)}) copy-start(bf16[384,384]{0,1:T(8,128)(2,1)} %copy-done.6) | copy-start | bytes 884740
  74.5 136.5 %reduce-scatter.7.cloned.1.call-start = ((), (), s32[]{:S(2)}) async-start(), calls=%async_computation.6 | async-start | bytes 1327104 | tf_op jit(solution)/shard_map/reduce_scatter | solution.py:128
  77.8 200.0 %reduce-scatter.9.cloned.1.call-start = ((), (), s32[]{:S(2)}) async-start(), calls=%async_computation.7 | async-start | bytes 1327104 | tf_op jit(solution)/shard_map/reduce_scatter | solution.py:131
  81.2 19.1 %copy-start.2 = (bf16[384,384]{0,1:T(8,128)(2,1)S(1)}, bf16[384,384]{0,1:T(8,128)(2,1)}, u32[]{:S(2)}) copy-start(bf16[384,384]{0,1:T(8,128)(2,1)} %copy-done.1) | copy-start | bytes 884740
  81.2 19.1 %copy-start.4 = (bf16[384,384]{0,1:T(8,128)(2,1)S(1)}, bf16[384,384]{0,1:T(8,128)(2,1)}, u32[]{:S(2)}) copy-start(bf16[384,384]{0,1:T(8,128)(2,1)} %copy-done.3) | copy-start | bytes 884740
  81.2 22.1 %copy-start.43 = (f32[384]{0:T(512)S(1)}, f32[384]{0:T(512)}, u32[]{:S(2)}) copy-start(f32[384]{0:T(512)} %get-tuple-element.50) | copy-start | bytes 4612
  81.2 22.6 %copy-start.42 = (f32[384]{0:T(512)S(1)}, f32[384]{0:T(512)}, u32[]{:S(2)}) copy-start(f32[384]{0:T(512)} %get-tuple-element.49) | copy-start | bytes 4612
  81.2 23.2 %copy-start.41 = (f32[384]{0:T(512)S(1)}, f32[384]{0:T(512)}, u32[]{:S(2)}) copy-start(f32[384]{0:T(512)} %get-tuple-element.51) | copy-start | bytes 4612
  81.2 23.8 %copy-start.40 = (f32[384]{0:T(512)S(1)}, f32[384]{0:T(512)}, u32[]{:S(2)}) copy-start(f32[384]{0:T(512)} %get-tuple-element.53) | copy-start | bytes 4612
  81.2 24.4 %copy-start.39 = (f32[384]{0:T(512)S(1)}, f32[384]{0:T(512)}, u32[]{:S(2)}) copy-start(f32[384]{0:T(512)} %get-tuple-element.52) | copy-start | bytes 4612
  81.2 24.9 %copy-start.38 = (f32[384]{0:T(512)S(1)}, f32[384]{0:T(512)}, u32[]{:S(2)}) copy-start(f32[384]{0:T(512)} %get-tuple-element.54) | copy-start | bytes 4612
  (8 other events, 17.8 us)
Sparse Core Ops, SparseCore 0:
  10.2 18.9 all-gather.2
  30.8 17.4 all-gather.4
  53.2 63.0 reduce-scatter.10
  118.7 26.7 reduce-scatter.12
  149.1 61.8 reduce-scatter.6
  214.7 63.0 reduce-scatter.8
where the time goes:
time: 291 us; the launch traced here: 286 us
  waiting for transfers between devices  141 us (48%)
  local copies, waits for them, and re-layouts  35.2 us (12%)
  blocking collectives  34.2 us (12%)
  other arithmetic  29.5 us (10%)
  matrix products  19.6 us (7%)
  between operations  14.8 us (5%)
  starting transfers between devices  12.1 us (4%)
    reduce_scatter x1, waiting for transfers between devices, on_device(): lax.psum_scatter(value_part.astype(jnp.bfloat16), 'frame', scatter_dimens...  50.4 us
    reduce_scatter x1, waiting for transfers between devices, on_device(): lax.psum_scatter(gate_part.astype(jnp.bfloat16), 'frame', scatter_dimensi...  37.2 us
    unnamed x7, waiting for transfers between devices  28.4 us
    psum x1, blocking collectives, on_device(): lax.psum((kernel_part, gain_part, bias_part), 'frame')  27.9 us
    another operation x32, local copies, waits for them, and re-layouts, on_device(): kernel_part = jnp.stack(kernel_rows)  21.5 us
    all_gather x1, waiting for transfers between devices, on_device(): full_inputs = lax.all_gather(inputs, 'chan', axis=0, tiled=True)  16.5 us
    unnamed x97, local copies, waits for them, and re-layouts  8.84 us
    reduce_sum x3, other arithmetic, on_device(): jnp.sum(grad_float * padded[:, k:k + frame_rows].astype(jnp.float32), axi...  7.63 us
  transfers between devices with their start and end apart: 10, of which 7 were waited for; matrix products, arithmetic and copies ran while one was open for 27% of the time, Pallas kernels for 0%

commit v1 on v0

v1 whole, which is shorter than its diff:
```python
import functools

import jax
import jax.numpy as jnp
from jax import lax
from jax.experimental import pallas as pl
from jax.experimental.pallas import tpu as pltpu
from jax.sharding import PartitionSpec as P

eps = 1e-05
pad = 16
row_tile = 64
MESH = pl.DeviceIdType.MESH
f32 = jnp.float32
bf16 = jnp.bfloat16


def dot(a, b, dims):
    return lax.dot_general(a, b, (dims, ((), ())), preferred_element_type=f32)


NN = ((1,), (0,))
NT = ((1,), (1,))


def kernel(
    n, F, x_ref, u_ref, gain_ref, bias_ref, vw_ref, gw_ref, w_ref, pw_ref, keep_ref,
    dx_ref, vg_ref, gg_ref, pg_ref, kg_ref, gb_ref,
    full_x, full_u, normed, vwt, gwt, vp, gs, gl_pad, cg_pad, act_t, conv_t, kacc,
    halo, snd1, rcv1, own1, snd2, rcv2,
    csnd1, crcv1, cown, csnd2, crcv2, st_snd, st_rcv, gb_snd, gb_rcv,
    k_snd, k_rcv1, k_snd2, k_rcv2,
    sx, rx, su, ru, sh, rh, s1, r1, s2, r2, sc1, rc1, sc2, rc2, sst, rst, sgb, rgb,
    sk1, rk1, sk2, rk2,
):
    C, T = x_ref.shape
    D = vw_ref.shape[1]
    taps = w_ref.shape[0]
    G = F // 2
    M = n // 2
    W = D // F
    me = lax.axis_index("chan")
    fr = lax.axis_index("frame")
    core = lax.rem(me, 2)
    chip = me // 2
    sib = me + 1 - 2 * core
    par = lax.rem(fr, 2)
    grp = fr // 2
    pair = fr + 1 - 2 * par
    pending = []

    def copy(src, dst, ssem, rsem, axis, index):
        return pltpu.make_async_remote_copy(
            src_ref=src, dst_ref=dst, send_sem=ssem, recv_sem=rsem,
            device_id={axis: index}, device_id_type=MESH,
        )

    def send(*args):
        c = copy(*args)
        c.start()
        pending.append(c)

    def rows(i, size):
        return pl.ds(pl.multiple_of(i * size, 16), size)

    barrier = pltpu.get_barrier_semaphore()
    for j in range(1, n):
        pl.semaphore_signal(
            barrier, inc=1, device_id={"chan": lax.rem(me + j, n)}, device_id_type=MESH
        )
    for j in range(1, F):
        pl.semaphore_signal(
            barrier, inc=1, device_id={"frame": lax.rem(fr + j, F)}, device_id_type=MESH
        )
    pl.semaphore_wait(barrier, n - 1 + F - 1)

    for ref, full, ss, rs in ((x_ref, full_x, sx, rx), (u_ref, full_u, su, ru)):
        for j in range(1, M):
            send(ref, full.at[rows(me, C)], ss.at[j], rs.at[me], "chan", lax.rem(me + 2 * j, n))
        send(ref, full.at[rows(me, C)], ss.at[0], rs.at[me], "chan", sib)
    full_x[rows(me, C), :] = x_ref[...]
    full_u[rows(me, C), :] = u_ref[...]
    vwt[...] = vw_ref[...].T
    gwt[...] = gw_ref[...].T

    def arrive(full, ss, rs, src):
        slot = full.at[rows(src, C)]
        copy(slot, slot, ss, rs.at[src], "chan", sib).wait_recv()

    def forward(full, ss, rs):
        for j in range(1, M):
            src = lax.rem(me + 2 * j, n)
            arrive(full, ss.at[0], rs, src)
            slot = full.at[rows(src, C)]
            send(slot, slot, ss.at[M + j - 1], rs.at[src], "chan", sib)

    def rest(full, ss, rs):
        for j in range(M):
            arrive(full, ss.at[0], rs, lax.rem(sib + 2 * j, n))

    forward(full_x, sx, rx)
    rest(full_x, sx, rx)
    total = jnp.zeros((1, T), f32)
    square = jnp.zeros((1, T), f32)
    for j in range(n):
        x = full_x[j * C : (j + 1) * C, :].astype(f32)
        total = total + jnp.sum(x, axis=0, keepdims=True)
        square = square + jnp.sum(x * x, axis=0, keepdims=True)
    mean = total / D
    inv_std = lax.rsqrt(square / D - mean * mean + eps)
    for j in range(n):
        x = full_x[j * C : (j + 1) * C, :].astype(f32)
        normed[j * C : (j + 1) * C, :] = (
            (x - mean) * inv_std * gain_ref[j] + bias_ref[j]
        ).astype(bf16)
    keep = keep_ref[...]
    vp[...] = dot(vw_ref[...], normed[...], NN)
    gs[...] = jax.nn.sigmoid(dot(gw_ref[...], normed[...], NN))
    glu = (vp[...] * gs[...] * keep).astype(bf16).astype(f32)
    gl_pad[0, pad : pad + T, :] = glu.T

    def edges(ref, which):
        right, left = lax.rem(fr + 1, F), lax.rem(fr + F - 1, F)
        a, b = 2 * which, 2 * which + 1
        send(ref.at[0, T : T + pad], halo.at[a], sh.at[a], rh.at[a], "frame", right)
        send(ref.at[0, pad : 2 * pad], halo.at[b], sh.at[b], rh.at[b], "frame", left)

    def edges_done(ref, which):
        a, b = 2 * which, 2 * which + 1
        copy(halo.at[a], halo.at[a], sh.at[a], rh.at[a], "frame", pair).wait_recv()
        copy(halo.at[b], halo.at[b], sh.at[b], rh.at[b], "frame", pair).wait_recv()
        ref[0, 0:pad, :] = jnp.where(fr > 0, halo[a], 0.0)
        ref[0, pad + T : T + 2 * pad, :] = jnp.where(fr < F - 1, halo[b], 0.0)
        span = T + 2 * pad - 8
        for p in range(1, 8):
            ref[p, 0:span, :] = ref[0, p : p + span, :]

    edges(gl_pad, 0)
    forward(full_u, su, ru)
    rest(full_u, su, ru)
    act_t[...] = dot(pw_ref[...], full_u[...], NN).astype(bf16).astype(f32).T
    edges_done(gl_pad, 0)

    lane_tile = 128 if C % 128 == 0 else C
    reach = taps // 2
    shift = pad - reach

    def window(ref, start, offset, lanes):
        return ref[offset % 8, pl.ds(start + offset // 8 * 8, row_tile), lanes]

    def conv_rows(i, carry):
        start = pl.multiple_of(i * row_tile, row_tile)
        for c0 in range(0, C, lane_tile):
            lanes = slice(c0, c0 + lane_tile)
            acc = jnp.zeros((row_tile, lane_tile), f32)
            for k in range(taps):
                acc = acc + w_ref[k : k + 1, lanes] * window(gl_pad, start, k + shift, lanes)
            s = jax.nn.sigmoid(acc)
            conv_t[pl.ds(start, row_tile), lanes] = (acc * s).astype(bf16)
            grad = act_t[pl.ds(start, row_tile), lanes] * (s + acc * s * (1.0 - s))
            cg_pad[0, pl.ds(start + pad, row_tile), lanes] = grad.astype(bf16).astype(f32)
        return carry

    lax.fori_loop(0, T // row_tile, conv_rows, 0)
    edges(cg_pad, 1)

    def part(arr, grad_of, fulls):
        for m in range(G):
            snd1[arr, m] = grad_of(fulls[rows(2 * m + 1 - par, W), :]).astype(bf16)
        send(snd1.at[arr], rcv1.at[arr], s1.at[arr], r1.at[arr], "frame", pair)

    def own_part(arr, grad_of, fulls):
        for m in range(G):
            own1[arr, m] = grad_of(fulls[rows(2 * m + par, W), :])

    def project_of(block):
        return dot(block, conv_t[...], NN)

    part(0, project_of, full_u)
    edges_done(cg_pad, 1)
    kacc[...] = jnp.zeros_like(kacc)

    def back_rows(i, carry):
        start = pl.multiple_of(i * row_tile, row_tile)
        for c0 in range(0, C, lane_tile):
            lanes = slice(c0, c0 + lane_tile)
            acc = jnp.zeros((row_tile, lane_tile), f32)
            here = window(cg_pad, start, pad, lanes)
            for k in range(taps):
                acc = acc + w_ref[k : k + 1, lanes] * window(cg_pad, start, pad + reach - k, lanes)
                prod = here * window(gl_pad, start, k + shift, lanes)
                kacc[8 * k : 8 * k + 8, lanes] += jnp.sum(
                    prod.reshape(row_tile // 8, 8, lane_tile), axis=0
                )
            act_t[pl.ds(start, row_tile), lanes] = acc
        return carry

    lax.fori_loop(0, T // row_tile, back_rows, 0)
    glu_grad = act_t[...].T * keep * gs[...]
    value_back = glu_grad.astype(bf16)
    gate_back = (glu_grad * vp[...] * (1.0 - gs[...])).astype(bf16)

    def value_of(block):
        return dot(block, value_back, NT)

    def gate_of(block):
        return dot(block, gate_back, NT)

    part(1, value_of, normed)

    def partial_term(j):
        return (
            dot(vwt[rows(j, C), :], value_back, NN) + dot(gwt[rows(j, C), :], gate_back, NN)
        ).astype(bf16)

    for m in range(M):
        csnd1[m] = partial_term(2 * m + 1 - core)
    send(csnd1, crcv1, sc1, rc1, "chan", sib)
    part(2, gate_of, normed)
    k_snd[...] = jnp.sum(kacc[...].reshape(kacc.shape[0] // 8, 8, C), axis=1)
    send(k_snd, k_rcv1, sk1, rk1, "frame", pair)
    for m in range(M):
        cown[m] = partial_term(2 * m + core)

    def second(arr):
        copy(snd1.at[arr], rcv1.at[arr], s1.at[arr], r1.at[arr], "frame", pair).wait_recv()
        for j in range(1, G):
            other = lax.rem(grp + j, G)
            snd2[arr, j] = (own1[arr, other] + rcv1[arr, other].astype(f32)).astype(bf16)
            send(
                snd2.at[arr, j], rcv2.at[arr, j], s2.at[arr, j], r2.at[arr, j],
                "frame", 2 * other + par,
            )

    own_part(0, project_of, full_u)
    second(0)

    copy(csnd1, crcv1, sc1, rc1, "chan", sib).wait_recv()
    for j in range(1, M):
        other = lax.rem(chip + j, M)
        csnd2[j] = (cown[other].astype(f32) + crcv1[other].astype(f32)).astype(bf16)
        send(
            csnd2.at[j], crcv2.at[j], sc2.at[j], rc2.at[j], "chan", 2 * other + core
        )
    own_part(1, value_of, normed)
    own_part(2, gate_of, normed)
    second(1)

    grad = cown[chip].astype(f32) + crcv1[chip].astype(f32)
    for j in range(1, M):
        copy(csnd2.at[j], crcv2.at[j], sc2.at[j], rc2.at[j], "chan", sib).wait_recv()
        grad = grad + crcv2[j].astype(f32)
    vp[...] = grad
    centred = (x_ref[...].astype(f32) - mean) * inv_std
    scaled = grad * gain_ref[me]
    st_snd[0:1, :] = jnp.sum(scaled, axis=0, keepdims=True)
    st_snd[1:2, :] = jnp.sum(scaled * centred, axis=0, keepdims=True)
    st_snd[2:8, :] = jnp.zeros((6, T), f32)
    for j in range(1, n):
        send(st_snd, st_rcv.at[j], sst.at[j], rst.at[j], "chan", lax.rem(me + j, n))
    gain_col = jnp.sum(grad * centred, axis=1, keepdims=True)
    bias_col = jnp.sum(grad, axis=1, keepdims=True)
    lane = lax.broadcasted_iota(jnp.int32, (C, 128), 1)
    gb_snd[...] = jnp.where(lane == 0, gain_col, bias_col).T[0:8, :]
    for j in range(1, F):
        send(gb_snd, gb_rcv.at[j], sgb.at[j], rgb.at[j], "frame", lax.rem(fr + j, F))

    copy(k_snd, k_rcv1, sk1, rk1, "frame", pair).wait_recv()
    k_snd2[...] = k_snd[...] + k_rcv1[...]
    for j in range(1, G):
        send(
            k_snd2, k_rcv2.at[j], sk2.at[j], rk2.at[j], "frame",
            2 * lax.rem(grp + j, G) + par,
        )
    second(2)

    stats = st_snd[...]
    for j in range(1, n):
        copy(st_snd, st_rcv.at[j], sst.at[j], rst.at[j], "chan", sib).wait_recv()
        stats = stats + st_rcv[j]
    stats = stats / D
    centred = (x_ref[...].astype(f32) - mean) * inv_std
    dx_ref[...] = (
        u_ref[...].astype(f32)
        + inv_std * (vp[...] * gain_ref[me] - stats[0:1, :] - centred * stats[1:2, :])
    ).astype(bf16)

    both = gb_snd[...]
    for j in range(1, F):
        copy(gb_snd, gb_rcv.at[j], sgb.at[j], rgb.at[j], "frame", pair).wait_recv()
        both = both + gb_rcv[j]
    gb_ref[...] = both
    taps_sum = k_snd2[...]
    for j in range(1, G):
        copy(k_snd2, k_rcv2.at[j], sk2.at[j], rk2.at[j], "frame", pair).wait_recv()
        taps_sum = taps_sum + k_rcv2[j]
    kg_ref[...] = taps_sum[0:taps, :]

    for arr, out in ((0, pg_ref), (1, vg_ref), (2, gg_ref)):
        acc = own1[arr, grp] + rcv1[arr, grp].astype(f32)
        for j in range(1, G):
            copy(
                snd2.at[arr, j], rcv2.at[arr, j], s2.at[arr, j], r2.at[arr, j], "frame", pair
            ).wait_recv()
            acc = acc + rcv2[arr, j].astype(f32)
        out[...] = acc.T

    for c in pending:
        c.wait_send()


def on_device(
    n, F, inputs, norm_gain, norm_bias, value_weight, gate_weight, conv_kernel,
    project_weight, frame_mask, upstream,
):
    C, T = inputs.shape
    D = value_weight.shape[1]
    taps = conv_kernel.shape[0]
    krows = -(-taps // 8) * 8
    G, M, W = F // 2, n // 2, D // F
    V = pltpu.VMEM
    S = pltpu.SemaphoreType.DMA
    scratch = [
        V((D, T), bf16), V((D, T), bf16), V((D, T), bf16), V((D, C), bf16), V((D, C), bf16),
        V((C, T), f32), V((C, T), f32), V((8, T + 2 * pad, C), f32), V((8, T + 2 * pad, C), f32),
        V((T, C), f32), V((T, C), bf16), V((8 * krows, C), f32),
        V((4, pad, C), f32),
        V((3, G, W, C), bf16), V((3, G, W, C), bf16), V((3, G, W, C), f32),
        V((3, G, W, C), bf16), V((3, G, W, C), bf16),
        V((M, C, T), bf16), V((M, C, T), bf16), V((M, C, T), bf16),
        V((M, C, T), bf16), V((M, C, T), bf16),
        V((8, T), f32), V((n, 8, T), f32), V((8, C), f32), V((F, 8, C), f32),
        V((krows, C), f32), V((krows, C), f32), V((krows, C), f32), V((G, krows, C), f32),
        S((n,)), S((n,)), S((n,)), S((n,)), S((4,)), S((4,)),
        S((3,)), S((3,)), S((3, G)), S((3, G)),
        S(()), S(()), S((M,)), S((M,)), S((n,)), S((n,)), S((F,)), S((F,)),
        S(()), S(()), S((G,)), S((G,)),
    ]
    out = jax.ShapeDtypeStruct
    vmem = pl.BlockSpec(memory_space=pltpu.VMEM)
    dx, vg, gg, pg, kg, gb = pl.pallas_call(
        functools.partial(kernel, n, F),
        out_shape=[
            out((C, T), bf16), out((C, W), f32), out((C, W), f32), out((C, W), f32),
            out((taps, C), f32), out((8, C), f32),
        ],
        in_specs=[vmem] * 9,
        out_specs=[vmem] * 6,
        scratch_shapes=scratch,
        compiler_params=pltpu.CompilerParams(
            collective_id=0, has_side_effects=True, vmem_limit_bytes=60 * 1024 * 1024
        ),
    )(
        inputs, upstream, norm_gain.reshape(n, C, 1), norm_bias.reshape(n, C, 1),
        value_weight, gate_weight, conv_kernel, project_weight,
        frame_mask.astype(f32)[None, :],
    )
    return dx, vg, gg, pg, kg, gb[0], gb[1]


def solution(mesh):
    return jax.shard_map(
        functools.partial(on_device, mesh.shape["chan"], mesh.shape["frame"]),
        mesh=mesh,
        in_specs=(
            P("chan", "frame"),
            P(),
            P(),
            P("chan", None),
            P("chan", None),
            P(None, "chan"),
            P("chan", None),
            P("frame"),
            P("chan", "frame"),
        ),
        out_specs=(
            P("chan", "frame"),
            P("chan", "frame"),
            P("chan", "frame"),
            P("chan", "frame"),
            P(None, "chan"),
            P("chan"),
            P("chan"),
        ),
        check_vma=False,
    )
```

time: 291 us -> 103 us (0.35); the launches traced: 286 us -> 102 us
  waiting for transfers between devices: 141 us -> 0 us
  Pallas kernels: 0 us -> 88.7 us
  blocking collectives: 34.2 us -> 0 us
  other arithmetic: 29.5 us -> 0.68 us
  local copies, waits for them, and re-layouts: 35.2 us -> 12.3 us
  matrix products: 19.6 us -> 0 us
  between operations: 14.8 us -> 0.66 us
  starting transfers between devices: 12.1 us -> 0 us
    reduce_scatter x3 -> x0, waiting for transfers between devices: 91.8 us -> none  [the longest x1 50.4 us: on_device(): lax.psum_scatter(value_part.astype(jnp.bfloat16), 'frame', scatter_dimens...]
    pallas_call x0 -> x1, Pallas kernels: none -> 88.7 us  [on_device(): pl.pallas_call(functools.partial(kernel, n, F), out_shape=[out((C, T), bf...]
    psum x2 -> x0, blocking collectives: 34.2 us -> none  [the longest x1 27.9 us: on_device(): lax.psum((kernel_part, gain_part, bias_part), 'frame')]
    unnamed x7 -> x0, waiting for transfers between devices: 28.4 us -> none
    another operation x32 -> x0, local copies, waits for them, and re-layouts: 21.5 us -> none  [on_device(): kernel_part = jnp.stack(kernel_rows)]
    dot_general x8 -> x0, matrix products: 19.6 us -> none  [the longest x1 3.82 us: on_device(): jnp.dot(project_weight, full_grads, preferred_element_type=jnp.float32)]
    all_gather x2 -> x0, waiting for transfers between devices: 16.5 us -> none  [the longest x1 16.5 us: on_device(): full_inputs = lax.all_gather(inputs, 'chan', axis=0, tiled=True)]
    convert_element_type x7 -> x1, other arithmetic: 12.5 us -> 0.68 us  [on_device(): frame_mask.astype(f32)[None, :]]
  transfers between devices with their start and end apart: 10 -> 0, of which waited for: 7 -> 0; matrix products, arithmetic and copies ran while one was open for 27% -> 0% of each run, Pallas kernels for 0% -> 0%
where the time goes in v1:
time: 103 us; the launch traced here: 102 us
  Pallas kernels  88.7 us (86%)
  local copies, waits for them, and re-layouts  12.3 us (12%)
    pallas_call x1, Pallas kernels, on_device(): pl.pallas_call(functools.partial(kernel, n, F), out_shape=[out((C, T), bf...  88.7 us
    unnamed x11, local copies, waits for them, and re-layouts  5.94 us
    reshape x1, local copies, waits for them, and re-layouts, on_device(): norm_bias.reshape(n, C, 1)  2.21 us
    reshape x1, local copies, waits for them, and re-layouts, on_device(): norm_gain.reshape(n, C, 1)  2.18 us

profile of v1, /device:TPU:9, one launch (start us, length us, event | category | flops | bytes accessed | tf_op | source)
XLA Modules:
  0.0 102.4 jit_solution(14504055789779980308)
XLA Ops:
  0.6 0.7 convert_element_type.3
  1.3 0.6 broadcast_in_dim.3.keep_ref
  1.9 2.2 %reshape.22.gain_ref = f32[4,384,1]{2,1,0:T(8,128)} reshape(f32[1536]{0:T(1024)} %param.10) | data formatting | bytes 12288 | tf_op jit(solution)/shard_map/reshape | solution.py:354
  4.1 2.2 %reshape.23.bias_ref = f32[4,384,1]{2,1,0:T(8,128)} reshape(f32[1536]{0:T(1024)} %param.11) | data formatting | bytes 12288 | tf_op jit(solution)/shard_map/reshape | solution.py:354
  6.3 88.7 %shard_map.144 = (bf16[384,384]{1,0:T(8,128)(2,1)}, f32[384,192]{1,0:T(8,128)}, f32[384,192]{1,0:T(8,128)}, f32[384,192]{1,0:T(8,128)}, f32[31,384]{1,0:T(8,128)}, /*index=5*/f32[8,384]{1,0:T(8,128)}) custom-call(bf16[384,384]{1,0:T(8,128)(2,1)} %x_ref.1, bf16[384,384]{1,0:T(8,128)(2,1)} %u_ref.1, f32[4,384,1]{2,1,0:T(8,128)} %reshape.22.gain_ref, ...), custom_call_target="tpu_custom_call" | custom-call | tf_op jit(solution)/shard_map/pallas_call | solution.py:341
  95.0 0.0 copy-start
  95.0 0.0 copy-start.1
  95.0 1.4 %slice_reduce_fusion = (f32[384]{0:T(512)}, f32[384]{0:T(512)}) fusion(f32[8,384]{1,0:T(8,128)} %get-tuple-element.18), kind=kLoop, calls=%fused_computation | loop fusion | bytes 6144 | tf_op jit(solution)/shard_map/slice | solution.py:358
  96.4 0.0 copy-start.2
  96.4 1.9 %copy.21 = f32[384,192]{0,1:T(8,128)} copy(f32[384,192]{1,0:T(8,128)} %get-tuple-element.27) | data formatting | bytes 589824
  98.3 1.9 %copy.22 = f32[384,192]{0,1:T(8,128)} copy(f32[384,192]{1,0:T(8,128)} %get-tuple-element.28) | data formatting | bytes 589824
  100.2 0.0 copy-done
  100.2 0.9 copy.23
  101.0 0.0 copy-done.1
  101.0 0.7 copy.26
  101.7 0.0 copy-done.2
  101.7 0.6 copy.27
Async XLA Ops:
  95.0 5.1 %copy-start = (f32[384,192]{1,0:T(8,128)S(1)}, f32[384,192]{1,0:T(8,128)}, u32[]{:S(2)}) copy-start(f32[384,192]{1,0:T(8,128)} %get-tuple-element.29) | copy-start | bytes 884740
  95.0 6.0 %copy-start.1 = (bf16[384,384]{1,0:T(8,128)(2,1)S(1)}, bf16[384,384]{1,0:T(8,128)(2,1)}, u32[]{:S(2)}) copy-start(bf16[384,384]{1,0:T(8,128)(2,1)} %get-tuple-element.42) | copy-start | bytes 884740
  96.4 5.3 %copy-start.2 = (f32[31,384]{1,0:T(8,128)S(1)}, f32[31,384]{1,0:T(8,128)}, u32[]{:S(2)}) copy-start(f32[31,384]{1,0:T(8,128)} %get-tuple-element.46) | copy-start | bytes 142852

commit v2 on v1

--- a/solution.py
+++ b/solution.py
@@ -30,7 +30,7 @@
     halo, snd1, rcv1, own1, snd2, rcv2,
     csnd1, crcv1, cown, csnd2, crcv2, st_snd, st_rcv, gb_snd, gb_rcv,
     k_snd, k_rcv1, k_snd2, k_rcv2,
-    sx, rx, su, ru, sh, rh, s1, r1, s2, r2, sc1, rc1, sc2, rc2, sst, rst, sgb, rgb,
+    gain_at, bias_at, sx, rx, su, ru, sh, rh, s1, r1, s2, r2, sc1, rc1, sc2, rc2, sst, rst, sgb, rgb,
     sk1, rk1, sk2, rk2,
 ):
     C, T = x_ref.shape
@@ -80,6 +80,8 @@
         send(ref, full.at[rows(me, C)], ss.at[0], rs.at[me], "chan", sib)
     full_x[rows(me, C), :] = x_ref[...]
     full_u[rows(me, C), :] = u_ref[...]
+    gain_at[...] = jnp.broadcast_to(gain_ref[...], (128, D)).T
+    bias_at[...] = jnp.broadcast_to(bias_ref[...], (128, D)).T
     vwt[...] = vw_ref[...].T
     gwt[...] = gw_ref[...].T
 
@@ -111,7 +113,8 @@
     for j in range(n):
         x = full_x[j * C : (j + 1) * C, :].astype(f32)
         normed[j * C : (j + 1) * C, :] = (
-            (x - mean) * inv_std * gain_ref[j] + bias_ref[j]
+            (x - mean) * inv_std * gain_at[j * C : (j + 1) * C, 0:1]
+            + bias_at[j * C : (j + 1) * C, 0:1]
         ).astype(bf16)
     keep = keep_ref[...]
     vp[...] = dot(vw_ref[...], normed[...], NN)
@@ -252,7 +255,7 @@
         grad = grad + crcv2[j].astype(f32)
     vp[...] = grad
     centred = (x_ref[...].astype(f32) - mean) * inv_std
-    scaled = grad * gain_ref[me]
+    scaled = grad * gain_at[rows(me, C), 0:1]
     st_snd[0:1, :] = jnp.sum(scaled, axis=0, keepdims=True)
     st_snd[1:2, :] = jnp.sum(scaled * centred, axis=0, keepdims=True)
     st_snd[2:8, :] = jnp.zeros((6, T), f32)
@@ -282,7 +285,7 @@
     centred = (x_ref[...].astype(f32) - mean) * inv_std
     dx_ref[...] = (
         u_ref[...].astype(f32)
-        + inv_std * (vp[...] * gain_ref[me] - stats[0:1, :] - centred * stats[1:2, :])
+        + inv_std * (vp[...] * gain_at[rows(me, C), 0:1] - stats[0:1, :] - centred * stats[1:2, :])
     ).astype(bf16)
 
     both = gb_snd[...]
@@ -303,7 +306,7 @@
                 snd2.at[arr, j], rcv2.at[arr, j], s2.at[arr, j], r2.at[arr, j], "frame", pair
             ).wait_recv()
             acc = acc + rcv2[arr, j].astype(f32)
-        out[...] = acc.T
+        out[...] = acc
 
     for c in pending:
         c.wait_send()
@@ -331,6 +334,7 @@
         V((M, C, T), bf16), V((M, C, T), bf16),
         V((8, T), f32), V((n, 8, T), f32), V((8, C), f32), V((F, 8, C), f32),
         V((krows, C), f32), V((krows, C), f32), V((krows, C), f32), V((G, krows, C), f32),
+        V((D, 128), f32), V((D, 128), f32),
         S((n,)), S((n,)), S((n,)), S((n,)), S((4,)), S((4,)),
         S((3,)), S((3,)), S((3, G)), S((3, G)),
         S(()), S(()), S((M,)), S((M,)), S((n,)), S((n,)), S((F,)), S((F,)),
@@ -341,7 +345,7 @@
     dx, vg, gg, pg, kg, gb = pl.pallas_call(
         functools.partial(kernel, n, F),
         out_shape=[
-            out((C, T), bf16), out((C, W), f32), out((C, W), f32), out((C, W), f32),
+            out((C, T), bf16), out((W, C), f32), out((W, C), f32), out((W, C), f32),
             out((taps, C), f32), out((8, C), f32),
         ],
         in_specs=[vmem] * 9,
@@ -351,11 +355,11 @@
             collective_id=0, has_side_effects=True, vmem_limit_bytes=60 * 1024 * 1024
         ),
     )(
-        inputs, upstream, norm_gain.reshape(n, C, 1), norm_bias.reshape(n, C, 1),
+        inputs, upstream, norm_gain[None, :], norm_bias[None, :],
         value_weight, gate_weight, conv_kernel, project_weight,
         frame_mask.astype(f32)[None, :],
     )
-    return dx, vg, gg, pg, kg, gb[0], gb[1]
+    return dx, vg.T, gg.T, pg.T, kg, gb[0], gb[1]
 
 
 def solution(mesh):

time: 103 us -> 99.6 us (0.967)
  local copies, waits for them, and re-layouts: 12.3 us -> 10 us
    reshape x2 -> x0, local copies, waits for them, and re-layouts: 4.39 us -> none  [the longest x1 2.21 us: on_device(): norm_bias.reshape(n, C, 1)]
    broadcast_in_dim x0 -> x2, local copies, waits for them, and re-layouts: none -> 2.59 us  [the longest x1 1.3 us: on_device(): norm_bias[None, :]]
where the time goes in v2:
time: 99.6 us; the launch traced here: 99.2 us
  Pallas kernels  87.8 us (88%)
  local copies, waits for them, and re-layouts  10 us (10%)
    pallas_call x1, Pallas kernels, on_device(): pl.pallas_call(functools.partial(kernel, n, F), out_shape=[out((C, T), bf...  87.8 us
    unnamed x11, local copies, waits for them, and re-layouts  5.46 us

profile of v2, /device:TPU:9, one launch (start us, length us, event | category | flops | bytes accessed | tf_op | source)
XLA Modules:
  0.0 99.2 jit_solution(9262539247591011998)
XLA Ops:
  0.6 1.3 %broadcast_in_dim.10.bias_ref = f32[1,1536]{1,0:T(1,128)} reshape(f32[1536]{0:T(1024)} %param.11) | data formatting | bytes 12288 | tf_op jit(solution)/shard_map/broadcast_in_dim | solution.py:358
  1.9 1.3 %broadcast_in_dim.9.gain_ref = f32[1,1536]{1,0:T(1,128)} reshape(f32[1536]{0:T(1024)} %param.10) | data formatting | bytes 12288 | tf_op jit(solution)/shard_map/broadcast_in_dim | solution.py:358
  3.2 0.7 convert_element_type.3
  3.9 0.6 broadcast_in_dim.11.keep_ref
  4.5 87.8 %shard_map.144 = (bf16[384,384]{1,0:T(8,128)(2,1)}, f32[192,384]{1,0:T(8,128)}, f32[192,384]{1,0:T(8,128)}, f32[192,384]{1,0:T(8,128)}, f32[31,384]{1,0:T(8,128)}, /*index=5*/f32[8,384]{1,0:T(8,128)}) custom-call(bf16[384,384]{1,0:T(8,128)(2,1)} %x_ref.1, bf16[384,384]{1,0:T(8,128)(2,1)} %u_ref.1, f32[1,1536]{1,0:T(1,128)} %broadcast_in_dim.9.gain_ref, ...), custom_call_target="tpu_custom_call" | custom-call | tf_op jit(solution)/shard_map/pallas_call | solution.py:345
  92.3 0.0 copy-start.1
  92.3 0.0 copy-start
  92.3 1.4 %slice_reduce_fusion = (f32[384]{0:T(512)}, f32[384]{0:T(512)}) fusion(f32[8,384]{1,0:T(8,128)} %get-tuple-element.18), kind=kLoop, calls=%fused_computation | loop fusion | bytes 6144 | tf_op jit(solution)/shard_map/slice | solution.py:362
  93.7 0.0 copy-start.2
  93.7 1.7 %copy.21 = bf16[384,384]{1,0:T(8,128)(2,1)} copy(bf16[384,384]{1,0:T(8,128)(2,1)} %get-tuple-element.28) | data formatting | bytes 589824
  95.4 1.7 %copy.22 = f32[384,192]{0,1:T(8,128)} copy(f32[384,192]{0,1:T(8,128)} %bitcast.5) | data formatting | bytes 589824
  97.1 0.0 copy-done.1
  97.1 0.7 copy.23
  97.8 0.0 copy-done
  97.8 0.7 copy.24
  98.6 0.0 copy-done.2
  98.6 0.6 copy.25
Async XLA Ops:
  92.3 4.8 %copy-start.1 = (f32[192,384]{1,0:T(8,128)S(1)}, f32[192,384]{1,0:T(8,128)}, u32[]{:S(2)}) copy-start(f32[192,384]{1,0:T(8,128)} %get-tuple-element.15) | copy-start | bytes 884740
  92.3 5.5 %copy-start = (f32[192,384]{1,0:T(8,128)S(1)}, f32[192,384]{1,0:T(8,128)}, u32[]{:S(2)}) copy-start(f32[192,384]{1,0:T(8,128)} %get-tuple-element.16) | copy-start | bytes 884740
  93.7 4.8 %copy-start.2 = (f32[31,384]{1,0:T(8,128)S(1)}, f32[31,384]{1,0:T(8,128)}, u32[]{:S(2)}) copy-start(f32[31,384]{1,0:T(8,128)} %get-tuple-element.32) | copy-start | bytes 142852

commit v3 on v2

--- a/solution.py
+++ b/solution.py
@@ -168,9 +168,14 @@
     edges(cg_pad, 1)
 
     def part(arr, grad_of, fulls):
-        for m in range(G):
+        for j in range(1, G + 1):
+            m = lax.rem(grp + j, G)
             snd1[arr, m] = grad_of(fulls[rows(2 * m + 1 - par, W), :]).astype(bf16)
-        send(snd1.at[arr], rcv1.at[arr], s1.at[arr], r1.at[arr], "frame", pair)
+            send(snd1.at[arr, m], rcv1.at[arr, m], s1.at[arr, j - 1], r1.at[arr, j - 1], "frame", pair)
+
+    def part_arrives(arr, j):
+        slot = rcv1.at[arr, lax.rem(grp + j, G)]
+        copy(slot, slot, s1.at[arr, j - 1], r1.at[arr, j - 1], "frame", pair).wait_recv()
 
     def own_part(arr, grad_of, fulls):
         for m in range(G):
@@ -226,8 +231,8 @@
         cown[m] = partial_term(2 * m + core)
 
     def second(arr):
-        copy(snd1.at[arr], rcv1.at[arr], s1.at[arr], r1.at[arr], "frame", pair).wait_recv()
         for j in range(1, G):
+            part_arrives(arr, j)
             other = lax.rem(grp + j, G)
             snd2[arr, j] = (own1[arr, other] + rcv1[arr, other].astype(f32)).astype(bf16)
             send(
@@ -300,6 +305,7 @@
     kg_ref[...] = taps_sum[0:taps, :]
 
     for arr, out in ((0, pg_ref), (1, vg_ref), (2, gg_ref)):
+        part_arrives(arr, G)
         acc = own1[arr, grp] + rcv1[arr, grp].astype(f32)
         for j in range(1, G):
             copy(
@@ -336,7 +342,7 @@
         V((krows, C), f32), V((krows, C), f32), V((krows, C), f32), V((G, krows, C), f32),
         V((D, 128), f32), V((D, 128), f32),
         S((n,)), S((n,)), S((n,)), S((n,)), S((4,)), S((4,)),
-        S((3,)), S((3,)), S((3, G)), S((3, G)),
+        S((3, G)), S((3, G)), S((3, G)), S((3, G)),
         S(()), S(()), S((M,)), S((M,)), S((n,)), S((n,)), S((F,)), S((F,)),
         S(()), S(()), S((G,)), S((G,)),
     ]

time: 99.6 us -> 99.1 us (level)
  no operation moved by 1% of the time
where the time goes in v3:
time: 99.1 us; the launch traced here: 98.7 us
  Pallas kernels  87.4 us (88%)
  local copies, waits for them, and re-layouts  10 us (10%)
    pallas_call x1, Pallas kernels, on_device(): pl.pallas_call(functools.partial(kernel, n, F), out_shape=[out((C, T), bf...  87.4 us
    unnamed x11, local copies, waits for them, and re-layouts  5.46 us

profile of v3, /device:TPU:9, one launch (start us, length us, event | category | flops | bytes accessed | tf_op | source)
XLA Modules:
  0.0 98.7 jit_solution(664821494667001368)
XLA Ops:
  0.6 1.3 %broadcast_in_dim.10.bias_ref = f32[1,1536]{1,0:T(1,128)} reshape(f32[1536]{0:T(1024)} %param.11) | data formatting | bytes 12288 | tf_op jit(solution)/shard_map/broadcast_in_dim | solution.py:364
  1.9 1.3 %broadcast_in_dim.9.gain_ref = f32[1,1536]{1,0:T(1,128)} reshape(f32[1536]{0:T(1024)} %param.10) | data formatting | bytes 12288 | tf_op jit(solution)/shard_map/broadcast_in_dim | solution.py:364
  3.2 0.7 convert_element_type.3
  3.9 0.6 broadcast_in_dim.11.keep_ref
  4.5 87.4 %shard_map.144 = (bf16[384,384]{1,0:T(8,128)(2,1)}, f32[192,384]{1,0:T(8,128)}, f32[192,384]{1,0:T(8,128)}, f32[192,384]{1,0:T(8,128)}, f32[31,384]{1,0:T(8,128)}, /*index=5*/f32[8,384]{1,0:T(8,128)}) custom-call(bf16[384,384]{1,0:T(8,128)(2,1)} %x_ref.1, bf16[384,384]{1,0:T(8,128)(2,1)} %u_ref.1, f32[1,1536]{1,0:T(1,128)} %broadcast_in_dim.9.gain_ref, ...), custom_call_target="tpu_custom_call" | custom-call | tf_op jit(solution)/shard_map/pallas_call | solution.py:351
  91.8 0.0 copy-start.1
  91.8 0.0 copy-start
  91.9 1.4 %slice_reduce_fusion = (f32[384]{0:T(512)}, f32[384]{0:T(512)}) fusion(f32[8,384]{1,0:T(8,128)} %get-tuple-element.18), kind=kLoop, calls=%fused_computation | loop fusion | bytes 6144 | tf_op jit(solution)/shard_map/slice | solution.py:368
  93.2 0.0 copy-start.2
  93.2 1.7 %copy.21 = bf16[384,384]{1,0:T(8,128)(2,1)} copy(bf16[384,384]{1,0:T(8,128)(2,1)} %get-tuple-element.28) | data formatting | bytes 589824
  94.9 1.7 %copy.22 = f32[384,192]{0,1:T(8,128)} copy(f32[384,192]{0,1:T(8,128)} %bitcast.5) | data formatting | bytes 589824
  96.6 0.0 copy-done.1
  96.6 0.7 copy.23
  97.4 0.0 copy-done
  97.4 0.7 copy.24
  98.1 0.0 copy-done.2
  98.1 0.6 copy.25
Async XLA Ops:
  91.8 4.8 %copy-start.1 = (f32[192,384]{1,0:T(8,128)S(1)}, f32[192,384]{1,0:T(8,128)}, u32[]{:S(2)}) copy-start(f32[192,384]{1,0:T(8,128)} %get-tuple-element.15) | copy-start | bytes 884740
  91.8 5.5 %copy-start = (f32[192,384]{1,0:T(8,128)S(1)}, f32[192,384]{1,0:T(8,128)}, u32[]{:S(2)}) copy-start(f32[192,384]{1,0:T(8,128)} %get-tuple-element.16) | copy-start | bytes 884740
  93.2 4.8 %copy-start.2 = (f32[31,384]{1,0:T(8,128)S(1)}, f32[31,384]{1,0:T(8,128)}, u32[]{:S(2)}) copy-start(f32[31,384]{1,0:T(8,128)} %get-tuple-element.32) | copy-start | bytes 142852
